TPU v7x, 512 devices: a whole 4x4x16 slice. The times are simulated.
512 devices in a mesh: lon: 8 (over y, z_hi), mem: 64 (over x, z_lo, core).
Axes of the slice: x: 4, y: 4, z: 16 (z_hi: 2, z_lo: 8; z = z_hi * 8 + z_lo), core: 2. Of those that a mesh axis runs over, the one named last changes fastest.
Arguments:
- ensemble: float32 [64, 98304], P('mem', 'lon')
- increments: bfloat16 [64, 98304], P('mem', 'lon'), may hold values from -6 to 6
- offsets: int32 [192, 7], P('lon'), may hold values from -12 to 12, as said below
- taper: bfloat16 [8, 512, 512], replicated
Outputs:
- covariance_product: float32 [64, 98304], P('mem', 'lon')
Inputs may be any that keep to these rules, and one draw needn't show every extreme that they name: Each row lists 7 different nonzero offsets in ascending order.
All inputs are finite; a program needn't handle non-finite values.
Results may differ from a plain program's by a relative error of at most 0.008.
Values may be sent and summed in bfloat16 or wider, within the bound.
A program may use at most 64 MiB of HBM per device.

v0:
```python
import jax
import jax.numpy as jnp
from jax import lax
from jax.sharding import PartitionSpec as P


def extended_2(block, sides, width):
    for axis, dim in sides:
        count = lax.axis_size(axis)
        forward = [(i, i + 1) for i in range(count - 1)]
        forward.append((count - 1, 0))
        backward = [(target, source) for source, target in forward]
        low = lax.ppermute(
            lax.slice_in_dim(block, block.shape[dim] - width, None, axis=dim), axis, forward
        )
        high = lax.ppermute(lax.slice_in_dim(block, 0, width, axis=dim), axis, backward)
        block = jnp.concatenate([low, block, high], axis=dim)
    return block


def taper_apply(extended, offsets, taper):
    vectors = extended.shape[0]
    block_count = offsets.shape[0]
    block_size = taper.shape[1]
    reach_blocks = block_count // 2
    blocks = extended.reshape(vectors, block_count + 2 * reach_blocks, block_size)
    block_rows = jnp.arange(block_count, dtype=jnp.int32) + reach_blocks
    indices = jnp.concatenate([block_rows[:, None], block_rows[:, None] + offsets], axis=1)
    picked = jnp.take(blocks, indices, axis=1)
    tapered = jnp.einsum("qrsb,sab->qra", picked, taper, preferred_element_type=jnp.float32)
    return tapered.reshape(vectors, block_count * block_size)


def extend_product(factor_one, factor_two, rim_width):
    weighted = (factor_one.astype(jnp.float32) * factor_two.astype(jnp.float32)).astype(
        jnp.bfloat16
    )
    return extended_2(weighted, (("lon", 1),), rim_width)


def on_device(ensemble, increments, offsets, taper):
    member_count = lax.axis_size("mem") * ensemble.shape[0]
    rim_width = offsets.shape[0] // 2 * taper.shape[1]
    ens_mean = lax.psum(jnp.sum(ensemble, axis=0), "mem") / member_count
    perturb = (ensemble - ens_mean[None, :]).astype(jnp.bfloat16)
    increments_all = lax.all_gather(increments, "mem", axis=0, tiled=True)
    extended = extend_product(perturb, increments_all, rim_width)
    tapered = taper_apply(extended, offsets, taper)
    summed = lax.psum_scatter(
        perturb.astype(jnp.float32) * tapered, "mem", scatter_dimension=0, tiled=True
    )
    return summed / (member_count - 1)


def solution(mesh):
    return jax.shard_map(
        on_device,
        mesh=mesh,
        in_specs=(P("mem", "lon"), P("mem", "lon"), P("lon", None), P()),
        out_specs=P("mem", "lon"),
        check_vma=False,
    )
```

profile of v0, /device:TPU:1, one launch (start us, length us, event | category | flops | bytes accessed | tf_op | source)
XLA Modules:
  0.0 1427.0 jit_solution(17073919097878806883)
XLA Ops:
  6.5 0.0 all-gather.3.cloned.1.call-start
  6.5 0.7 all-gather.3.cloned.1.call-update
  7.3 0.0 all-reduce.3.cloned.1.call-start
  7.3 504.5 %psum.7 = f32[12288]{0:T(1024)S(1)} all-reduce(f32[12288]{0:T(1024)} %bitcast.42), channel_id=1, replica_groups=mesh['lon'=8,'mem'=64] {'mem'}, use_global_device_ids=true, to_apply=%region_0.0 | all-reduce | flops 12288 | bytes 98304 | tf_op jit(solution)/shard_map/psum | solution.py:44
  511.9 0.8 convert_convert_fusion
  512.7 0.0 all-gather.3.cloned.1.call-done
  512.7 0.0 copy-start
  512.7 3.6 fusion.6
  516.4 1.3 fusion.14
  517.7 7.0 collective-permute-start
  524.7 9.1 collective-permute-start.1
  533.8 0.0 copy-done
  533.9 0.1 copy.22
  533.9 0.1 reshape.98
  534.1 0.1 copy.19
  534.2 15.4 %collective-permute-done = bf16[64,6144]{1,0:T(8,128)(2,1)S(1)} collective-permute-done((bf16[64,6144]{1,0:T(8,128)(2,1)}, bf16[64,6144]{1,0:T(8,128)(2,1)S(1)}, u32[]{:S(2)}, u32[]{:S(2)}) %collective-permute-start) | collective-permute-done | bytes 786464 | tf_op jit(solution)/shard_map/ppermute | solution.py:13
  549.6 15.8 %collective-permute-done.1 = bf16[64,6144]{1,0:T(8,128)(2,1)S(1)} collective-permute-done((bf16[64,6144]{1,0:T(8,128)(2,1)}, bf16[64,6144]{1,0:T(8,128)(2,1)S(1)}, u32[]{:S(2)}, u32[]{:S(2)}) %collective-permute-start.1) | collective-permute-done | bytes 786464 | tf_op jit(solution)/shard_map/ppermute | solution.py:16
  565.4 0.2 pad_maximum_fusion
  565.6 0.4 copy.30
  566.0 8.2 gather_fusion
  574.2 10.6 fusion.7
  584.8 0.3 copy.27
  585.2 1.9 broadcast_multiply_fusion
  587.1 0.0 all-reduce.3.cloned.1.call-update
  587.1 1.3 dynamic-slice
  588.5 829.3 %all-reduce.3.cloned.1.call-done = f32[64,12288]{1,0:T(8,128)} async-done(((f32[64,12288]{1,0:T(8,128)}), f32[64,12288]{1,0:T(8,128)}) %all-reduce.3.cloned.1.call-update) | async-done | bytes 3145744
  1417.8 2.4 dynamic-slice_multiply_fusion
  (9 shorter events, 0.1 us)
Async XLA Ops:
  6.5 506.2 %all-gather.3.cloned.1.call-start = ((), (), s32[]{:S(2)}) async-start(), calls=%async_computation | async-start | bytes 3194880 | tf_op jit(solution)/shard_map/all_gather | solution.py:46
  7.3 1410.5 %all-reduce.3.cloned.1.call-start = ((), (), s32[]{:S(2)}) async-start(), calls=%async_computation.1 | async-start | bytes 6291456
  512.7 21.1 %copy-start = (s32[24,7]{0,1:T(8,128)S(1)}, s32[24,7]{0,1:T(8,128)}, u32[]{:S(2)}) copy-start(s32[24,7]{0,1:T(8,128)} %param.6) | copy-start | bytes 2020
  517.7 31.9 %collective-permute-start = (bf16[64,6144]{1,0:T(8,128)(2,1)}, bf16[64,6144]{1,0:T(8,128)(2,1)S(1)}, u32[]{:S(2)}, u32[]{:S(2)}) collective-permute-start(bf16[64,6144]{1,0:T(8,128)(2,1)} %get-tuple-element.5), channel_id=1, source_target_pairs={{0,64},{64,128},{128,192},{192,256},{256,320},{320,384},{384,448},... | collective-permute-start | bytes 2359304 | tf_op jit(solution)/shard_map/ppermute | solution.py:13
  524.7 40.6 %collective-permute-start.1 = (bf16[64,6144]{1,0:T(8,128)(2,1)}, bf16[64,6144]{1,0:T(8,128)(2,1)S(1)}, u32[]{:S(2)}, u32[]{:S(2)}) collective-permute-start(bf16[64,6144]{1,0:T(8,128)(2,1)} %get-tuple-element.6), channel_id=1, source_target_pairs={{64,0},{128,64},{192,128},{256,192},{320,256},{384,320},{448,384},... | collective-permute-start | bytes 2359304 | tf_op jit(solution)/shard_map/ppermute | solution.py:16
Sparse Core Ops, SparseCore 0:
  9.5 127.7 all-gather.2
  587.3 830.4 all-reduce.2
where the time goes:
time: 1430 us
  waiting for transfers between devices  861 us (60%)
  blocking collectives  505 us (35%)
  starting transfers between devices  16.1 us (1%)
    unnamed x3, waiting for transfers between devices  830 us
    psum x1, blocking collectives, on_device(): ens_mean = lax.psum(jnp.sum(ensemble, axis=0), 'mem') / member_count  505 us
  transfers between devices with their start and end apart: 4, of which 3 were waited for; matrix products, arithmetic and copies ran while one was open for 0% of the time, Pallas kernels for 0%

commit v1 on v0

v1 whole, which is shorter than its diff:
```python
import functools

import jax
import jax.numpy as jnp
from jax import lax
from jax.experimental import pallas as pl
from jax.experimental.pallas import tpu as pltpu
from jax.sharding import PartitionSpec as P

MESH = pl.DeviceIdType.MESH
F32, BF16 = jnp.float32, jnp.bfloat16
NT = (((1,), (1,)), ((), ()))

X, Z, CORES = 4, 8, 2
ROW = X * CORES
LON = 8
RING = 2 * Z
BLOCKS, SLOTS, BLOCK, LANES = 24, 8, 512, 128
Q = BLOCK // LANES
INNER = BLOCKS * Q
RIM = INNER // 2
EXT = INNER + 2 * RIM
PART = EXT // ROW
CHUNK = 8
CHUNKS = BLOCKS // CHUNK
CROWS = CHUNK * Q
MEMBERS = X * Z * CORES


def kernel(
    ens, inc, off, tap_hbm, out,
    ebuf, dbuf, ring, yhalo, incf, mu, muin, delta, w, wd, tap, outf, outb, red,
    tsem, es, er, hs, hr, fs, fr, rs, rr, ls, lr, ys, yr, ms, mr, ds_, dr, os_, or_,
):
    lon, mem = lax.axis_index("lon"), lax.axis_index("mem")
    x, zlo, core = mem // (Z * CORES), (mem // CORES) % Z, mem % CORES
    y, zhi = lon // 2, lon % 2
    r = x * CORES + core
    z = zhi * Z + zlo

    def row_peer(d):
        rr_ = (r + d) % ROW
        return (lon, (rr_ // CORES) * (Z * CORES) + zlo * CORES + rr_ % CORES)

    def col_peer(d):
        return (lon, x * (Z * CORES) + ((zlo + d) % Z) * CORES + core)

    def ring_peer(d):
        zz = (z + d + RING) % RING
        return (y * 2 + zz // Z, x * (Z * CORES) + (zz % Z) * CORES + core)

    def lon_peer(d):
        return ((lon + d + LON) % LON, mem)

    y_to = lon_peer(2 - 4 * zhi)

    def copy(src, dst, ssem, rsem, dev):
        return pltpu.make_async_remote_copy(
            src_ref=src, dst_ref=dst, send_sem=ssem, recv_sem=rsem,
            device_id=dev, device_id_type=MESH,
        )

    tap_copy = pltpu.make_async_copy(tap_hbm, tap, tsem)
    tap_copy.start()

    barrier = pltpu.get_barrier_semaphore()
    peers = [row_peer(d) for d in range(1, ROW)] + [col_peer(d) for d in range(1, Z)]
    peers += [ring_peer(1), ring_peer(-1)]
    peers += [lon_peer(d) for d in (1, -1, 2, -2)]
    for dev in peers:
        pl.semaphore_signal(barrier, inc=1, device_id=dev, device_id_type=MESH)
    pl.semaphore_wait(barrier, len(peers))

    def erow(row, lo, n):
        return ebuf.at[pl.ds(pl.multiple_of(row * EXT + lo, 8), n)]

    halo_lo = copy(ens.at[pl.ds(RIM, RIM)], erow(r, 0, RIM), hs.at[0], hr.at[0], lon_peer(1))
    halo_hi = copy(ens.at[pl.ds(0, RIM)], erow(r, RIM + INNER, RIM), hs.at[1], hr.at[1], lon_peer(-1))
    halo_lo.start()
    halo_hi.start()

    def right(t):
        slot = (z - t + RING) % RING
        src = inc if t == 0 else ring.at[slot]
        return copy(src, ring.at[slot], rs.at[t], rr.at[t], ring_peer(1))

    def left(t):
        slot = (z + t) % RING
        src = inc if t == 0 else ring.at[slot]
        return copy(src, ring.at[slot], ls.at[t], lr.at[t], ring_peer(-1))

    right(0).start()
    left(0).start()
    inner = [copy(ens, erow(r, RIM, INNER), es.at[d], er.at[d], row_peer(d)) for d in range(1, ROW)]
    for c in inner:
        c.start()
    ebuf[pl.ds(pl.multiple_of(r * EXT + RIM, 8), INNER), :] = ens[...]
    ring[z] = inc[...]

    fwd = []
    for side, lo in ((0, 0), (1, RIM + INNER)):
        for d in range(1, ROW):
            fwd.append(copy(erow(r, lo, RIM), erow(r, lo, RIM), fs.at[side, d], fr.at[side, d], row_peer(d)))

    y_lo = pl.multiple_of((1 - zhi) * RIM, 16)

    def y_copy(k, slot):
        return copy(ring.at[slot, pl.ds(y_lo, RIM)], yhalo.at[k], ys.at[k], yr.at[k], y_to)

    def on_y(slot):
        @pl.when(slot // Z != zhi)
        def _():
            y_copy(slot % Z, slot).start()

    for t in range(RING // 2):
        slot = (z - 1 - t + RING) % RING
        copy(ring.at[slot], ring.at[slot], rs.at[t], rr.at[t], ring_peer(1)).wait_recv()
        if t < RING // 2 - 1:
            right(t + 1).start()
        on_y(slot)
        if t < RING // 2 - 1:
            slot = (z + 1 + t) % RING
            copy(ring.at[slot], ring.at[slot], ls.at[t], lr.at[t], ring_peer(-1)).wait_recv()
            if t < RING // 2 - 2:
                left(t + 1).start()
            on_y(slot)
        if t == 2:
            halo_lo.wait_recv()
            for c in fwd[: ROW - 1]:
                c.start()
            halo_hi.wait_recv()
            for c in fwd[ROW - 1 :]:
                c.start()

    for d in range(1, ROW):
        src = (r - d + ROW) % ROW
        copy(ens, erow(src, RIM, INNER), es.at[d], er.at[d], row_peer(d)).wait_recv()
        for side, lo in ((0, 0), (1, RIM + INNER)):
            copy(erow(src, lo, RIM), erow(src, lo, RIM), fs.at[side, d], fr.at[side, d], row_peer(d)).wait_recv()

    step = 32

    def differences(i, _):
        at = pl.multiple_of(i * step, step)
        rows = [ebuf[pl.ds(pl.multiple_of(m * EXT + at, 8), step), :] for m in range(ROW)]
        mean = functools.reduce(jnp.add, rows) * (1.0 / ROW)
        mu[pl.ds(at, step), :] = mean
        for m in range(ROW):
            dbuf[pl.ds(pl.multiple_of(m * EXT + at, 8), step), :] = rows[m] - mean
        return 0

    lax.fori_loop(0, EXT // step, differences, 0)

    part = pl.multiple_of(r * PART, 8)
    means = [copy(mu.at[pl.ds(part, PART)], muin.at[zlo], ms.at[d], mr.at[d], col_peer(d)) for d in range(1, Z)]
    for c in means:
        c.start()
    muin[zlo] = mu[pl.ds(part, PART), :]

    def widen(k, _):
        base = k * EXT
        incf[pl.ds(pl.multiple_of(base + RIM, 8), INNER), :] = ring[zhi * Z + k].astype(F32)
        near = pl.multiple_of(base + (1 - zhi) * (RIM + INNER), 8)
        incf[pl.ds(near, RIM), :] = ring[(1 - zhi) * Z + k, pl.ds(pl.multiple_of(zhi * RIM, 16), RIM), :].astype(F32)
        return 0

    lax.fori_loop(0, Z, widen, 0)
    for k in range(Z):
        y_copy(k, k).wait_recv()

    def widen_y(k, _):
        far = pl.multiple_of(k * EXT + zhi * (RIM + INNER), 8)
        incf[pl.ds(far, RIM), :] = yhalo[k].astype(F32)
        return 0

    lax.fori_loop(0, Z, widen_y, 0)

    def weigh(j, _):
        for q in range(Q):
            dq = dbuf[pl.ds(j * Q + q, ROW, stride=EXT), :]
            iq = incf[pl.ds(j * Q + q, Z, stride=EXT), :]
            rows = jnp.concatenate([dq[m : m + 1] * iq for m in range(ROW)], axis=0)
            w[j, :, q * LANES : (q + 1) * LANES] = rows.astype(BF16)
        return 0

    lax.fori_loop(0, 2 * BLOCKS, weigh, 0)

    for d in range(1, Z):
        src = (zlo - d + Z) % Z
        copy(mu.at[pl.ds(part, PART)], muin.at[src], ms.at[d], mr.at[d], col_peer(d)).wait_recv()
    total = functools.reduce(jnp.add, [muin[k] for k in range(Z)])
    delta[pl.ds(part, PART), :] = mu[pl.ds(part, PART), :] - total * (1.0 / Z)
    shifts = [copy(delta.at[pl.ds(part, PART)], delta.at[pl.ds(part, PART)], ds_.at[d], dr.at[d], row_peer(d)) for d in range(1, ROW)]
    for c in shifts:
        c.start()
    tap_copy.wait()

    def block_of(i, s):
        j = i + BLOCKS // 2
        return j if s == 0 else j + off[i, s - 1]

    def shift_pass():
        for d in range(1, ROW):
            src = pl.multiple_of(((r - d + ROW) % ROW) * PART, 8)
            copy(delta.at[pl.ds(src, PART)], delta.at[pl.ds(src, PART)], ds_.at[d], dr.at[d], row_peer(d)).wait_recv()

        def weigh_shift(j, _):
            for q in range(Q):
                iq = incf[pl.ds(j * Q + q, Z, stride=EXT), :]
                wd[j, :, q * LANES : (q + 1) * LANES] = delta[pl.ds(j * Q + q, 1), :] * iq
            return 0

        lax.fori_loop(0, 2 * BLOCKS, weigh_shift, 0)
        acc = None
        for s in range(SLOTS):
            lhs = jnp.concatenate([wd[block_of(i, s)] for i in range(BLOCKS)], axis=0).astype(BF16)
            part_ = lax.dot_general(lhs, tap[s], NT, preferred_element_type=F32)
            acc = part_ if acc is None else acc + part_
        for i in range(BLOCKS):
            for q in range(Q):
                shift = delta[pl.ds(RIM + i * Q + q, 1), :] * float(ROW)
                outf[pl.ds(i * Q + q, Z, stride=INNER), :] = (
                    shift * acc[i * Z : (i + 1) * Z, q * LANES : (q + 1) * LANES]
                )

    def product(c, _):
        i0 = c * CHUNK
        acc = None
        for s in range(SLOTS):
            lhs = jnp.concatenate([w[block_of(i0 + b, s)] for b in range(CHUNK)], axis=0)
            part_ = lax.dot_general(lhs, tap[s], NT, preferred_element_type=F32)
            acc = part_ if acc is None else acc + part_

        pl.when(c == 0)(shift_pass)

        for b in range(CHUNK):
            for q in range(Q):
                at = (i0 + b) * Q + q
                dq = dbuf[pl.ds(RIM + at, ROW, stride=EXT), :]
                o = outf[pl.ds(at, Z, stride=INNER), :]
                for m in range(ROW):
                    lo = (b * ROW + m) * Z
                    o += dq[m : m + 1] * acc[lo : lo + Z, q * LANES : (q + 1) * LANES]
                outf[pl.ds(at, Z, stride=INNER), :] = o
        rows = pl.multiple_of(c * CROWS, CROWS)
        for k in range(Z):
            outb[k, pl.ds(rows, CROWS), :] = outf[pl.ds(pl.multiple_of(k * INNER + rows, 8), CROWS), :].astype(BF16)
        for d in range(1, Z):
            send(c, d).start()
        return 0

    def send(c, d):
        rows = pl.ds(pl.multiple_of(c * CROWS, CROWS), CROWS)
        return copy(outb.at[(zlo + d) % Z, rows], red.at[zlo, rows], os_.at[c, d], or_.at[c, d], col_peer(d))

    lax.fori_loop(0, CHUNKS, product, 0)

    own = outf[pl.ds(pl.multiple_of(zlo * INNER, 8), INNER), :]
    for d in range(1, Z):
        src = (zlo - d + Z) % Z
        for c in range(CHUNKS):
            rows = pl.ds(c * CROWS, CROWS)
            copy(outb.at[src, rows], red.at[src, rows], os_.at[c, d], or_.at[c, d], col_peer(d)).wait_recv()
        own += red[src].astype(F32)
    out[...] = own / (MEMBERS - 1)

    for c in [halo_lo, halo_hi] + inner + fwd + means + shifts:
        c.wait_send()
    for t in range(RING // 2):
        right(t).wait_send()
        if t < RING // 2 - 1:
            left(t).wait_send()
    for k in range(Z):
        y_copy(k, k).wait_send()
    for c in range(CHUNKS):
        for d in range(1, Z):
            send(c, d).wait_send()


def on_device(ensemble, increments, offsets, taper):
    ens = ensemble.reshape(INNER, LANES)
    inc = increments.reshape(INNER, LANES)
    dma = pltpu.SemaphoreType.DMA
    vmem = pl.BlockSpec(memory_space=pltpu.VMEM)
    out = pl.pallas_call(
        kernel,
        out_shape=jax.ShapeDtypeStruct((INNER, LANES), F32),
        in_specs=[vmem, vmem, pl.BlockSpec(memory_space=pltpu.SMEM), pl.BlockSpec(memory_space=pl.ANY)],
        out_specs=vmem,
        scratch_shapes=[
            pltpu.VMEM((ROW * EXT, LANES), F32),
            pltpu.VMEM((ROW * EXT, LANES), F32),
            pltpu.VMEM((RING, INNER, LANES), BF16),
            pltpu.VMEM((Z, RIM, LANES), BF16),
            pltpu.VMEM((Z * EXT, LANES), F32),
            pltpu.VMEM((EXT, LANES), F32),
            pltpu.VMEM((Z, PART, LANES), F32),
            pltpu.VMEM((EXT, LANES), F32),
            pltpu.VMEM((2 * BLOCKS, ROW * Z, BLOCK), BF16),
            pltpu.VMEM((2 * BLOCKS, Z, BLOCK), F32),
            pltpu.VMEM((SLOTS, BLOCK, BLOCK), BF16),
            pltpu.VMEM((Z * INNER, LANES), F32),
            pltpu.VMEM((Z, INNER, LANES), BF16),
            pltpu.VMEM((Z, INNER, LANES), BF16),
            dma,
            dma((ROW,)), dma((ROW,)),
            dma((2,)), dma((2,)),
            dma((2, ROW)), dma((2, ROW)),
            dma((RING // 2,)), dma((RING // 2,)),
            dma((RING // 2,)), dma((RING // 2,)),
            dma((Z,)), dma((Z,)),
            dma((Z,)), dma((Z,)),
            dma((ROW,)), dma((ROW,)),
            dma((CHUNKS, Z)), dma((CHUNKS, Z)),
        ],
        compiler_params=pltpu.CompilerParams(
            collective_id=0, has_side_effects=True, vmem_limit_bytes=48 << 20
        ),
        name="covariance",
    )(ens, inc, offsets, taper)
    return out.reshape(1, INNER * LANES)


def solution(mesh):
    return jax.shard_map(
        on_device,
        mesh=mesh,
        in_specs=(P("mem", "lon"), P("mem", "lon"), P("lon", None), P()),
        out_specs=P("mem", "lon"),
        check_vma=False,
    )
```

time: 1430 us -> 76.3 us (0.05)
  waiting for transfers between devices: 861 us -> 0 us
  blocking collectives: 505 us -> 0 us
  Pallas kernels: 0 us -> 70.7 us
  starting transfers between devices: 16.1 us -> 0 us
    unnamed x3 -> x0, waiting for transfers between devices: 830 us -> none
    psum x1 -> x0, blocking collectives: 505 us -> none  [on_device(): ens_mean = lax.psum(jnp.sum(ensemble, axis=0), 'mem') / member_count]
    pallas_call x0 -> x1, Pallas kernels: none -> 70.7 us  [on_device(): pl.pallas_call(kernel, out_shape=jax.ShapeDtypeStruct((INNER, LANES), F32...]
    ppermute x2 -> x0, waiting for transfers between devices: 31.2 us -> none  [the longest x1 15.8 us: extended_2(): lax.ppermute(lax.slice_in_dim(block, 0, width, axis=dim), axis, backward)]
    ppermute x2 -> x0, starting transfers between devices: 16.1 us -> none  [the longest x1 9.06 us: extended_2(): lax.ppermute(lax.slice_in_dim(block, 0, width, axis=dim), axis, backward)]
  transfers between devices with their start and end apart: 4 -> 0, of which waited for: 3 -> 0; matrix products, arithmetic and copies ran while one was open for 0% -> 0% of each run, Pallas kernels for 0% -> 0%
where the time goes in v1:
time: 76.3 us; the launch traced here: 76 us
  Pallas kernels  70.7 us (93%)
  local copies, waits for them, and re-layouts  4.37 us (6%)
  other arithmetic  0.93 us (1%)
    pallas_call x1, Pallas kernels, on_device(): pl.pallas_call(kernel, out_shape=jax.ShapeDtypeStruct((INNER, LANES), F32...  70.7 us
    unnamed x6, local copies, waits for them, and re-layouts  4.37 us

profile of v1, /device:TPU:1, one launch (start us, length us, event | category | flops | bytes accessed | tf_op | source)
XLA Modules:
  0.0 76.0 jit_solution(11203131571681894484)
XLA Ops:
  0.0 0.8 %copy.5.off = s32[24,7]{1,0:T(8,128)S(1)} copy(s32[24,7]{0,1:T(8,128)} %param.6) | data formatting | bytes 1344 | tf_op args[2]
  0.8 0.9 %reduce = bf16[12288]{0:T(1024)(128)(2,1)S(1)} reduce(bf16[1,12288]{1,0:T(2,128)(2,1)} %param.5, bf16[]{:T(256)} %constant.2), dimensions={0}, to_apply=%param.5.reduce_sub_computation | reduce | bytes 49154 | tf_op args[1]
  1.7 0.0 copy-start
  1.7 2.2 %copy-done = bf16[8,512,512]{2,1,0:T(8,128)(2,1)S(1)} copy-done((bf16[8,512,512]{2,1,0:T(8,128)(2,1)S(1)}, bf16[8,512,512]{2,1,0:T(8,128)(2,1)}, u32[]{:S(2)}) %copy-start) | copy-done | bytes 4194328
  3.9 0.0 copy-start.1
  3.9 0.8 %copy-done.1 = f32[1,12288]{1,0:T(1,128)S(1)} copy-done((f32[1,12288]{1,0:T(1,128)S(1)}, f32[1,12288]{1,0:T(1,128)}, u32[]{:S(2)}) %copy-start.1) | copy-done | bytes 49176
  4.7 70.7 %covariance.1 = f32[96,128]{1,0:T(8,128)S(1)} custom-call(f32[96,128]{1,0:T(8,128)S(1)} %bitcast.5, bf16[96,128]{1,0:T(8,128)(2,1)S(1)} %bitcast.4, s32[24,7]{1,0:T(8,128)S(1)} %copy.5.off, bf16[8,512,512]{2,1,0:T(8,128)(2,1)S(1)} %copy-done), custom_call_target="tpu_custom_call" | custom-call | tf_op jit(solution)/shard_map/covariance/pallas_call | solution.py:285
  75.4 0.6 copy.7
Async XLA Ops:
  1.7 2.2 %copy-start = (bf16[8,512,512]{2,1,0:T(8,128)(2,1)S(1)}, bf16[8,512,512]{2,1,0:T(8,128)(2,1)}, u32[]{:S(2)}) copy-start(bf16[8,512,512]{2,1,0:T(8,128)(2,1)} %tap_hbm.1) | copy-start | bytes 12582916
  3.9 0.8 %copy-start.1 = (f32[1,12288]{1,0:T(1,128)S(1)}, f32[1,12288]{1,0:T(1,128)}, u32[]{:S(2)}) copy-start(f32[1,12288]{1,0:T(1,128)} %param.4) | copy-start | bytes 147460

commit v2 on v0

v2 whole, which is shorter than its diff:
```python
import functools

import jax
import jax.numpy as jnp
from jax import lax
from jax.experimental import pallas as pl
from jax.experimental.pallas import tpu as pltpu
from jax.sharding import PartitionSpec as P

MESH = pl.DeviceIdType.MESH
F32, BF16 = jnp.float32, jnp.bfloat16
NT = (((1,), (1,)), ((), ()))

X, Z, CORES = 4, 8, 2
ROW = X * CORES
HALF = Z // 2
LON = 8
RING = 2 * Z
BLOCKS, SLOTS, BLOCK, LANES = 24, 8, 512, 128
Q = BLOCK // LANES
INNER = BLOCKS * Q
RIM = INNER // 2
EXT = INNER + 2 * RIM
PART = 16
PARTS = INNER // PART
CHUNK = 8
CHUNKS = BLOCKS // CHUNK
CROWS = CHUNK * Q
MEMBERS = X * Z * CORES


def kernel(
    ens, inc, off, tap_hbm, out,
    eb, ib, db, incf, df, mus, mi, dsend, dlt, w, wd, tap, outf, outb, red,
    hello, tsem, es, er, is_, ir, hs, hr, fs, fr, ds_, dr, ms, mr, ss, sr, bs, br, os_, or_,
):
    lon, mem = lax.axis_index("lon"), lax.axis_index("mem")
    x, zlo, core = mem // (Z * CORES), (mem // CORES) % Z, mem % CORES
    zhi = lon % 2
    r = x * CORES + core
    g = x * 2 + zlo % 2
    zq = zlo // 2
    mine = core * HALF + zq

    def rank(zz):
        return jnp.minimum(zz, Z)

    rank_me = rank(zhi * Z + zlo)

    def row_peer(d):
        rr_ = (r + d) % ROW
        return (lon, (rr_ // CORES) * (Z * CORES) + zlo * CORES + rr_ % CORES)

    def set_peer(d):
        gg = (g + d) % ROW
        return (lon, (gg // 2) * (Z * CORES) + (zq * 2 + gg % 2) * CORES + core)

    def far_peer(dl, d):
        zt = (zlo + d) % Z
        half = zhi if dl == 0 else 1 - zhi
        dev = ((lon + dl + LON) % LON, x * (Z * CORES) + zt * CORES + core)
        return dev, rank(half * Z + zt)

    far = [(dl, d, *far_peer(dl, d)) for dl in (0, 1, -1) for d in range(Z) if dl or d]

    def copy(src, dst, ssem, rsem, dev):
        return pltpu.make_async_remote_copy(
            src_ref=src, dst_ref=dst, send_sem=ssem, recv_sem=rsem,
            device_id=dev, device_id_type=MESH,
        )

    tap_copy = pltpu.make_async_copy(tap_hbm, tap, tsem)
    tap_copy.start()

    barrier = pltpu.get_barrier_semaphore()
    for d in range(1, ROW):
        pl.semaphore_signal(barrier, inc=1, device_id=row_peer(d), device_id_type=MESH)
    for d in range(1, ROW):
        pl.semaphore_signal(barrier, inc=1, device_id=set_peer(d), device_id_type=MESH)
    before, after = 2 * (ROW - 1), [0, 0]
    for dl, _, dev, rk in far:

        @pl.when(rk >= rank_me)
        def _():
            pl.semaphore_signal(barrier, inc=1, device_id=dev, device_id_type=MESH)

        before += (rk <= rank_me).astype(jnp.int32)
        after[abs(dl)] += (rk > rank_me).astype(jnp.int32)
    pl.semaphore_wait(barrier, before)
    for dl, _, dev, rk in far:

        @pl.when(rk < rank_me)
        def _():
            pl.semaphore_signal(hello.at[abs(dl)], inc=1, device_id=dev, device_id_type=MESH)

    def wait_hello(n):
        pl.when(after[n] > 0)(lambda: pl.semaphore_wait(hello.at[n], after[n]))

    def ecopy(d, src):
        return copy(ens, eb.at[src], es.at[d], er.at[d], row_peer(d))

    def icopy(d, src):
        return copy(inc, ib.at[src, pl.ds(RIM, INNER)], is_.at[d], ir.at[d], set_peer(d))

    def ihalo(dl):
        n, lo, to = (0, RIM, 0) if dl == 1 else (1, 0, RIM + INNER)
        return copy(inc.at[pl.ds(lo, RIM)], ib.at[g, pl.ds(to, RIM)], hs.at[n], hr.at[n], far_peer(dl, 0)[0])

    def ifwd(n, d, src):
        rim = ib.at[src, pl.ds(n * (RIM + INNER), RIM)]
        return copy(rim, rim, fs.at[n, d], fr.at[n, d], set_peer(d))

    def dcopy(dl, d, src, dev):
        n, lo, to, rows = {0: (0, RIM, RIM, INNER), 1: (1, 2 * RIM, 0, RIM), -1: (2, RIM, RIM + INNER, RIM)}[dl]
        row = core * HALF + src
        return copy(db.at[row, pl.ds(lo, rows)], db.at[row, pl.ds(to, rows)], ds_.at[n, d // 2], dr.at[n, src], dev)

    def bcopy(n, side):
        lo, rows = ((RIM, INNER), (0, RIM), (RIM + INNER, RIM))[n]
        half = db.at[pl.ds(side * HALF, HALF), pl.ds(lo, rows)]
        return copy(half, half, bs.at[n], br.at[n], (lon, mem + 1 - 2 * core))

    part = pl.multiple_of((r % PARTS) * PART, PART)

    def mcopy(n, d, src, dev):
        return copy(mus.at[pl.ds(part, PART)], mi.at[n, src], ms.at[n, d], mr.at[n, src], dev)

    has_part = {0: r < PARTS, 1: (r >= PARTS // 2) & (r < PARTS), -1: r < PARTS // 2}

    def scopy(d, src):
        there = pl.ds(pl.multiple_of(((r + d) % ROW // CORES * 2 + zlo % 2) * 2 * PART, 2 * PART), 2 * PART)
        here = pl.ds(pl.multiple_of((src % PARTS) * 2 * PART, 2 * PART), 2 * PART)
        return copy(dsend.at[there], dlt.at[here], ss.at[d], sr.at[src], row_peer(d))

    def ocopy(c, d, src):
        rows = pl.ds(pl.multiple_of(c * CROWS, CROWS), CROWS)
        return copy(outb.at[(g + d) % ROW, rows], red.at[src, rows], os_.at[c, d], or_.at[c, src], set_peer(d))

    for d in range(1, ROW):
        ecopy(d, r).start()
    for dl in (1, -1):
        pl.when(far_peer(dl, 0)[1] <= rank_me)(lambda dl=dl: ihalo(dl).start())
    for d in range(1, ROW):
        icopy(d, g).start()
    eb[r] = ens[...]
    ib[g, pl.ds(RIM, INNER), :] = inc[...]

    for d in range(1, ROW):
        ecopy(d, (r - d + ROW) % ROW).wait_recv()
    mean = functools.reduce(jnp.add, [eb[k] for k in range(ROW)]) * (1.0 / ROW)
    mus[...] = mean
    db[mine, pl.ds(RIM, INNER), :] = (ens[...] - mean).astype(BF16)

    def send_far(late, dls):
        def due(rk):
            return (rk > rank_me) if late else (rk <= rank_me)

        for dl, d, dev, rk in far:
            if dl in dls and d % 2 == 0:
                pl.when(due(rk))(lambda: dcopy(dl, d, zq, dev).start())
        for dl, d, dev, rk in far:
            if dl in dls:
                pl.when(due(rk) & has_part[dl])(lambda: mcopy(abs(dl), d, zlo, dev).start())

    send_far(False, (1, -1))
    send_far(False, (0,))
    wait_hello(0)
    send_far(True, (0,))
    wait_hello(1)
    for dl in (1, -1):
        pl.when(far_peer(dl, 0)[1] > rank_me)(lambda dl=dl: ihalo(dl).start())
    send_far(True, (1, -1))

    @pl.when(has_part[0])
    def _():
        mi[0, zlo] = mus[pl.ds(part, PART), :]

    ihalo(1).wait_recv()
    for d in range(1, ROW):
        ifwd(0, d, g).start()
    ihalo(-1).wait_recv()
    for d in range(1, ROW):
        ifwd(1, d, g).start()
    for k in range(HALF):
        pl.when(k != zq)(lambda k=k: dcopy(0, 0, k, far[0][2]).wait_recv())
    bcopy(0, core).start()
    for d in range(1, ROW):
        icopy(d, (g - d + ROW) % ROW).wait_recv()
    tap_copy.wait()
    for n in range(2):
        for d in range(1, ROW):
            ifwd(n, d, (g - d + ROW) % ROW).wait_recv()

    def widen(src, dst, lo, n):
        def one(k, _):
            dst[pl.ds(pl.multiple_of(k * EXT, EXT), EXT), :] = src[k].astype(F32)
            return 0

        lax.fori_loop(lo, lo + n, one, 0)

    widen(ib, incf, 0, ROW)
    for dl in (1, -1):
        for k in range(HALF):
            dcopy(dl, 0, k, far[0][2]).wait_recv()
        bcopy(1 if dl == 1 else 2, core).start()
    widen(db, df, core * HALF, HALF)
    for n in range(3):
        bcopy(n, 1 - core).wait_recv()
    widen(db, df, (1 - core) * HALF, HALF)

    @pl.when(has_part[0])
    def _():
        for k in range(Z):
            pl.when(k != zlo)(lambda k=k: mcopy(0, 0, k, far[0][2]).wait_recv())
            mcopy(1, 0, k, far[0][2]).wait_recv()
        for n in range(2):
            whole = functools.reduce(jnp.add, [mi[n, k] for k in range(Z)]) * (1.0 / Z)
            for k in range(Z):
                dsend[k * 2 * PART + n * PART : k * 2 * PART + (n + 1) * PART, :] = mi[n, k] - whole
        here = pl.ds(pl.multiple_of((r % PARTS) * 2 * PART, 2 * PART), 2 * PART)
        dlt[here, :] = dsend[pl.ds(pl.multiple_of(g * 2 * PART, 2 * PART), 2 * PART), :]
        for d in range(1, ROW):
            scopy(d, r).start()

    def weigh(j, _):
        for q in range(Q):
            dq = df[pl.ds(j * Q + q, Z, stride=EXT), :]
            iq = incf[pl.ds(j * Q + q, ROW, stride=EXT), :]
            rows = jnp.concatenate([dq[m : m + 1] * iq for m in range(Z)], axis=0)
            w[j, :, q * LANES : (q + 1) * LANES] = rows.astype(BF16)
        return 0

    lax.fori_loop(0, 2 * BLOCKS, weigh, 0)

    def shift_row(j, q):
        b = (j + BLOCKS // 2) % BLOCKS
        rim = (j < BLOCKS // 2) | (j >= BLOCKS + BLOCKS // 2)
        rim = int(rim) if isinstance(j, int) else rim.astype(jnp.int32)
        return (b // Q) * 2 * PART + rim * PART + (b % Q) * Q + q

    def block_of(i, s):
        j = i + BLOCKS // 2
        return j if s == 0 else j + off[s - 1, i]

    def shift_pass():
        for k in range(PARTS):
            pl.when(k != r)(lambda k=k: scopy(1, k).wait_recv())

        def weigh_shift(j, _):
            for q in range(Q):
                iq = incf[pl.ds(j * Q + q, ROW, stride=EXT), :]
                wd[j, :, q * LANES : (q + 1) * LANES] = dlt[pl.ds(shift_row(j, q), 1), :] * iq
            return 0

        lax.fori_loop(0, 2 * BLOCKS, weigh_shift, 0)
        acc = None
        for s in range(SLOTS):
            lhs = jnp.concatenate([wd[block_of(i, s)] for i in range(BLOCKS)], axis=0).astype(BF16)
            part_ = lax.dot_general(lhs, tap[s], NT, preferred_element_type=F32)
            acc = part_ if acc is None else acc + part_
        for i in range(BLOCKS):
            for q in range(Q):
                shift = dlt[pl.ds(shift_row(i + BLOCKS // 2, q), 1), :] * float(ROW)
                outf[pl.ds(i * Q + q, ROW, stride=INNER), :] = (
                    shift * acc[i * ROW : (i + 1) * ROW, q * LANES : (q + 1) * LANES]
                )

    def product(c, _):
        i0 = c * CHUNK
        acc = None
        for s in range(SLOTS):
            lhs = jnp.concatenate([w[block_of(i0 + b, s)] for b in range(CHUNK)], axis=0)
            part_ = lax.dot_general(lhs, tap[s], NT, preferred_element_type=F32)
            acc = part_ if acc is None else acc + part_

        pl.when(c == 0)(shift_pass)

        for b in range(CHUNK):
            for q in range(Q):
                at = (i0 + b) * Q + q
                dq = df[pl.ds(RIM + at, Z, stride=EXT), :]
                o = outf[pl.ds(at, ROW, stride=INNER), :]
                for m in range(Z):
                    lo = (b * Z + m) * ROW
                    o += dq[m : m + 1] * acc[lo : lo + ROW, q * LANES : (q + 1) * LANES]
                outf[pl.ds(at, ROW, stride=INNER), :] = o
        rows = pl.multiple_of(c * CROWS, CROWS)
        for k in range(ROW):
            outb[k, pl.ds(rows, CROWS), :] = outf[pl.ds(pl.multiple_of(k * INNER + rows, 8), CROWS), :].astype(BF16)
        for d in range(1, ROW):
            ocopy(c, d, g).start()
        return 0

    lax.fori_loop(0, CHUNKS, product, 0)

    own = outf[pl.ds(pl.multiple_of(g * INNER, 8), INNER), :]
    for d in range(1, ROW):
        src = (g - d + ROW) % ROW
        for c in range(CHUNKS):
            ocopy(c, d, src).wait_recv()
        own += red[src].astype(F32)
    out[...] = own / (MEMBERS - 1)

    for d in range(1, ROW):
        ecopy(d, r).wait_send()
        icopy(d, g).wait_send()
        for n in range(2):
            ifwd(n, d, g).wait_send()
        for c in range(CHUNKS):
            ocopy(c, d, g).wait_send()
    for dl in (1, -1):
        ihalo(dl).wait_send()
    for n in range(3):
        bcopy(n, core).wait_send()
    for dl, d, dev, _ in far:
        if d % 2 == 0:
            dcopy(dl, d, zq, dev).wait_send()
        pl.when(has_part[dl])(lambda: mcopy(abs(dl), d, zlo, dev).wait_send())

    @pl.when(has_part[0])
    def _():
        for d in range(1, ROW):
            scopy(d, r).wait_send()


def on_device(ensemble, increments, offsets, taper):
    ens = ensemble.reshape(INNER, LANES)
    inc = increments.reshape(INNER, LANES)
    dma = pltpu.SemaphoreType.DMA
    vmem = pl.BlockSpec(memory_space=pltpu.VMEM)
    out = pl.pallas_call(
        kernel,
        out_shape=jax.ShapeDtypeStruct((INNER, LANES), F32),
        in_specs=[vmem, vmem, pl.BlockSpec(memory_space=pltpu.SMEM), pl.BlockSpec(memory_space=pltpu.HBM)],
        out_specs=vmem,
        scratch_shapes=[
            pltpu.VMEM((ROW, INNER, LANES), F32),
            pltpu.VMEM((ROW, EXT, LANES), BF16),
            pltpu.VMEM((Z, EXT, LANES), BF16),
            pltpu.VMEM((ROW * EXT, LANES), F32),
            pltpu.VMEM((Z * EXT, LANES), F32),
            pltpu.VMEM((INNER, LANES), F32),
            pltpu.VMEM((2, Z, PART, LANES), F32),
            pltpu.VMEM((Z * 2 * PART, LANES), F32),
            pltpu.VMEM((PARTS * 2 * PART, LANES), F32),
            pltpu.VMEM((2 * BLOCKS, Z * ROW, BLOCK), BF16),
            pltpu.VMEM((2 * BLOCKS, ROW, BLOCK), F32),
            pltpu.VMEM((SLOTS, BLOCK, BLOCK), BF16),
            pltpu.VMEM((ROW * INNER, LANES), F32),
            pltpu.VMEM((ROW, INNER, LANES), BF16),
            pltpu.VMEM((ROW, INNER, LANES), BF16),
            pltpu.SemaphoreType.REGULAR((2,)),
            dma,
            dma((ROW,)), dma((ROW,)),
            dma((ROW,)), dma((ROW,)),
            dma((2,)), dma((2,)),
            dma((2, ROW)), dma((2, ROW)),
            dma((3, HALF)), dma((3, HALF)),
            dma((2, Z)), dma((2, Z)),
            dma((ROW,)), dma((ROW,)),
            dma((3,)), dma((3,)),
            dma((CHUNKS, ROW)), dma((CHUNKS, ROW)),
        ],
        compiler_params=pltpu.CompilerParams(
            collective_id=0, has_side_effects=True, vmem_limit_bytes=121 << 19
        ),
        name="covariance",
    )(ens, inc, offsets.T, taper)
    return out.reshape(1, INNER * LANES)


def solution(mesh):
    return jax.shard_map(
        on_device,
        mesh=mesh,
        in_specs=(P("mem", "lon"), P("mem", "lon"), P("lon", None), P()),
        out_specs=P("mem", "lon"),
        check_vma=False,
    )
```

time: 1430 us -> 65.9 us (0.05)
  waiting for transfers between devices: 861 us -> 0 us
  blocking collectives: 505 us -> 0 us
  Pallas kernels: 0 us -> 62.6 us
  starting transfers between devices: 16.1 us -> 0 us
    unnamed x3 -> x0, waiting for transfers between devices: 830 us -> none
    psum x1 -> x0, blocking collectives: 505 us -> none  [on_device(): ens_mean = lax.psum(jnp.sum(ensemble, axis=0), 'mem') / member_count]
    pallas_call x0 -> x1, Pallas kernels: none -> 62.6 us  [on_device(): pl.pallas_call(kernel, out_shape=jax.ShapeDtypeStruct((INNER, LANES), F32...]
    ppermute x2 -> x0, waiting for transfers between devices: 31.2 us -> none  [the longest x1 15.8 us: extended_2(): lax.ppermute(lax.slice_in_dim(block, 0, width, axis=dim), axis, backward)]
    ppermute x2 -> x0, starting transfers between devices: 16.1 us -> none  [the longest x1 9.06 us: extended_2(): lax.ppermute(lax.slice_in_dim(block, 0, width, axis=dim), axis, backward)]
  transfers between devices with their start and end apart: 4 -> 0, of which waited for: 3 -> 0; matrix products, arithmetic and copies ran while one was open for 0% -> 0% of each run, Pallas kernels for 0% -> 0%
where the time goes in v2:
time: 65.9 us; the launch traced here: 65.6 us
  Pallas kernels  62.6 us (95%)
  other arithmetic  1.54 us (2%)
  local copies, waits for them, and re-layouts  1.42 us (2%)
    pallas_call x1, Pallas kernels, on_device(): pl.pallas_call(kernel, out_shape=jax.ShapeDtypeStruct((INNER, LANES), F32...  62.6 us
    unnamed x1, other arithmetic  1.54 us
    unnamed x1, local copies, waits for them, and re-layouts  1.42 us

profile of v2, /device:TPU:1, one launch (start us, length us, event | category | flops | bytes accessed | tf_op | source)
XLA Modules:
  0.0 65.6 jit_solution(4042726016724572689)
XLA Ops:
  0.0 1.5 %reduce = bf16[12288]{0:T(1024)(128)(2,1)} reduce(bf16[1,12288]{1,0:T(2,128)(2,1)} %param.5, bf16[]{:T(256)} %constant.2), dimensions={0}, to_apply=%param.5.reduce_sub_computation | reduce | bytes 49154 | tf_op args[1]
  1.5 62.6 %covariance.1 = f32[96,128]{1,0:T(8,128)} custom-call(f32[96,128]{1,0:T(8,128)} %bitcast.6, bf16[96,128]{1,0:T(8,128)(2,1)} %bitcast.5, s32[7,24]{1,0:T(8,128)} %bitcast.7, bf16[8,512,512]{2,1,0:T(8,128)(2,1)} %tap_hbm.1), custom_call_target="tpu_custom_call" | custom-call | tf_op jit(solution)/shard_map/covariance/pallas_call | solution.py:331
  64.2 1.4 %copy.6 = f32[1,12288]{1,0:T(1,128)} copy(f32[1,12288]{1,0:T(1,128)} %bitcast.4) | data formatting | bytes 98304

commit v3 on v2

--- a/solution.py
+++ b/solution.py
@@ -31,7 +31,7 @@
 
 def kernel(
     ens, inc, off, tap_hbm, out,
-    eb, ib, db, incf, df, mus, mi, dsend, dlt, w, wd, tap, outf, outb, red,
+    eb, ib, db, incf, df, mus, mi, dsend, dlt, w, wd, tacc, tap, outf, outb, red,
     hello, tsem, es, er, is_, ir, hs, hr, fs, fr, ds_, dr, ms, mr, ss, sr, bs, br, os_, or_,
 ):
     lon, mem = lax.axis_index("lon"), lax.axis_index("mem")
@@ -75,9 +75,10 @@
     barrier = pltpu.get_barrier_semaphore()
     for d in range(1, ROW):
         pl.semaphore_signal(barrier, inc=1, device_id=row_peer(d), device_id_type=MESH)
-    for d in range(1, ROW):
-        pl.semaphore_signal(barrier, inc=1, device_id=set_peer(d), device_id_type=MESH)
-    before, after = 2 * (ROW - 1), [0, 0]
+    for k in range(X):
+        dev = (lon, k * (Z * CORES) + (zq * 2 + 1 - zlo % 2) * CORES + core)
+        pl.semaphore_signal(barrier, inc=1, device_id=dev, device_id_type=MESH)
+    before, after = ROW - 1 + X, [0, 0]
     for dl, _, dev, rk in far:
 
         @pl.when(rk >= rank_me)
@@ -87,12 +88,6 @@
         before += (rk <= rank_me).astype(jnp.int32)
         after[abs(dl)] += (rk > rank_me).astype(jnp.int32)
     pl.semaphore_wait(barrier, before)
-    for dl, _, dev, rk in far:
-
-        @pl.when(rk < rank_me)
-        def _():
-            pl.semaphore_signal(hello.at[abs(dl)], inc=1, device_id=dev, device_id_type=MESH)
-
     def wait_hello(n):
         pl.when(after[n] > 0)(lambda: pl.semaphore_wait(hello.at[n], after[n]))
 
@@ -138,12 +133,18 @@
 
     for d in range(1, ROW):
         ecopy(d, r).start()
+    for dl, _, dev, rk in far:
+
+        @pl.when(rk < rank_me)
+        def _():
+            pl.semaphore_signal(hello.at[abs(dl)], inc=1, device_id=dev, device_id_type=MESH)
     for dl in (1, -1):
         pl.when(far_peer(dl, 0)[1] <= rank_me)(lambda dl=dl: ihalo(dl).start())
     for d in range(1, ROW):
         icopy(d, g).start()
     eb[r] = ens[...]
     ib[g, pl.ds(RIM, INNER), :] = inc[...]
+    outf[...] = jnp.zeros_like(outf)
 
     for d in range(1, ROW):
         ecopy(d, (r - d + ROW) % ROW).wait_recv()
@@ -191,25 +192,60 @@
         for d in range(1, ROW):
             ifwd(n, d, (g - d + ROW) % ROW).wait_recv()
 
-    def widen(src, dst, lo, n):
+    def widen(src, dst, k0, n, lo, rows):
         def one(k, _):
-            dst[pl.ds(pl.multiple_of(k * EXT, EXT), EXT), :] = src[k].astype(F32)
+            dst[pl.ds(pl.multiple_of(k * EXT + lo, PART), rows), :] = src[k, pl.ds(lo, rows), :].astype(F32)
             return 0
 
-        lax.fori_loop(lo, lo + n, one, 0)
-
-    widen(ib, incf, 0, ROW)
+        lax.fori_loop(k0, k0 + n, one, 0)
+
+    def weigh(j, _):
+        for q in range(Q):
+            dq = df[pl.ds(j * Q + q, ROW, stride=EXT), :]
+            iq = incf[pl.ds(j * Q + q, ROW, stride=EXT), :]
+            rows = jnp.concatenate([dq[m : m + 1] * iq for m in range(ROW)], axis=0)
+            w[j, :, q * LANES : (q + 1) * LANES] = rows.astype(BF16)
+        return 0
+
+    widen(ib, incf, 0, ROW, 0, EXT)
+    bcopy(0, 1 - core).wait_recv()
+    widen(db, df, 0, ROW, RIM, INNER)
+    lax.fori_loop(BLOCKS // 2, BLOCKS + BLOCKS // 2, weigh, 0)
+
+    def block_of(i, s):
+        j = i + BLOCKS // 2
+        return j if s == 0 else j + off[s - 1, i]
+
+    def through(first, count, s):
+        lhs = jnp.concatenate([w[block_of(first + b, s)] for b in range(count)], axis=0)
+        whole = lax.dot_general(lhs, tap[s], NT, preferred_element_type=F32)
+        return whole.reshape(count, ROW * ROW, BLOCK)
+
+    def own_tile(c, _):
+        tacc[pl.ds(c * CHUNK, CHUNK)] = through(c * CHUNK, CHUNK, 0)
+        return 0
+
+    lax.fori_loop(0, CHUNKS, own_tile, 0)
+    mid = range(CHUNK, 2 * CHUNK)
+    late = []
+    for s in range(1, SLOTS):
+        inner = [i for i in mid if BLOCKS // 2 + 1 - s <= i <= BLOCKS // 2 + 6 - s]
+        tacc[pl.ds(inner[0], len(inner))] += through(inner[0], len(inner), s)
+        late += [(mid[0], inner[0] - mid[0], s), (inner[-1] + 1, mid[-1] - inner[-1], s)]
+
     for dl in (1, -1):
         for k in range(HALF):
             dcopy(dl, 0, k, far[0][2]).wait_recv()
         bcopy(1 if dl == 1 else 2, core).start()
-    widen(db, df, core * HALF, HALF)
-    for n in range(3):
+    widen(db, df, core * HALF, HALF, 0, RIM)
+    widen(db, df, core * HALF, HALF, RIM + INNER, RIM)
+    for n in (1, 2):
         bcopy(n, 1 - core).wait_recv()
-    widen(db, df, (1 - core) * HALF, HALF)
-
-    @pl.when(has_part[0])
-    def _():
+        lo = (n - 1) * (RIM + INNER)
+        widen(db, df, (1 - core) * HALF, HALF, lo, RIM)
+        lax.fori_loop(lo // Q, lo // Q + BLOCKS // 2, weigh, 0)
+
+    def shift_start():
         for k in range(Z):
             pl.when(k != zlo)(lambda k=k: mcopy(0, 0, k, far[0][2]).wait_recv())
             mcopy(1, 0, k, far[0][2]).wait_recv()
@@ -222,25 +258,11 @@
         for d in range(1, ROW):
             scopy(d, r).start()
 
-    def weigh(j, _):
-        for q in range(Q):
-            dq = df[pl.ds(j * Q + q, Z, stride=EXT), :]
-            iq = incf[pl.ds(j * Q + q, ROW, stride=EXT), :]
-            rows = jnp.concatenate([dq[m : m + 1] * iq for m in range(Z)], axis=0)
-            w[j, :, q * LANES : (q + 1) * LANES] = rows.astype(BF16)
-        return 0
-
-    lax.fori_loop(0, 2 * BLOCKS, weigh, 0)
-
     def shift_row(j, q):
         b = (j + BLOCKS // 2) % BLOCKS
         rim = (j < BLOCKS // 2) | (j >= BLOCKS + BLOCKS // 2)
         rim = int(rim) if isinstance(j, int) else rim.astype(jnp.int32)
         return (b // Q) * 2 * PART + rim * PART + (b % Q) * Q + q
-
-    def block_of(i, s):
-        j = i + BLOCKS // 2
-        return j if s == 0 else j + off[s - 1, i]
 
     def shift_pass():
         for k in range(PARTS):
@@ -261,37 +283,50 @@
         for i in range(BLOCKS):
             for q in range(Q):
                 shift = dlt[pl.ds(shift_row(i + BLOCKS // 2, q), 1), :] * float(ROW)
-                outf[pl.ds(i * Q + q, ROW, stride=INNER), :] = (
+                outf[pl.ds(i * Q + q, ROW, stride=INNER), :] += (
                     shift * acc[i * ROW : (i + 1) * ROW, q * LANES : (q + 1) * LANES]
                 )
 
-    def product(c, _):
-        i0 = c * CHUNK
-        acc = None
-        for s in range(SLOTS):
-            lhs = jnp.concatenate([w[block_of(i0 + b, s)] for b in range(CHUNK)], axis=0)
-            part_ = lax.dot_general(lhs, tap[s], NT, preferred_element_type=F32)
-            acc = part_ if acc is None else acc + part_
-
-        pl.when(c == 0)(shift_pass)
-
+    def emit(c, _):
+        rows = pl.multiple_of(c * CROWS, CROWS)
+        for k in range(ROW):
+            outb[k, pl.ds(rows, CROWS), :] = outf[pl.ds(pl.multiple_of(k * INNER + rows, 8), CROWS), :].astype(BF16)
+        for d in range(1, ROW):
+            ocopy(c, d, g).start()
+        return 0
+
+    def finish(c, acc):
         for b in range(CHUNK):
             for q in range(Q):
-                at = (i0 + b) * Q + q
+                at = (c * CHUNK + b) * Q + q
                 dq = df[pl.ds(RIM + at, Z, stride=EXT), :]
                 o = outf[pl.ds(at, ROW, stride=INNER), :]
                 for m in range(Z):
                     lo = (b * Z + m) * ROW
                     o += dq[m : m + 1] * acc[lo : lo + ROW, q * LANES : (q + 1) * LANES]
                 outf[pl.ds(at, ROW, stride=INNER), :] = o
-        rows = pl.multiple_of(c * CROWS, CROWS)
-        for k in range(ROW):
-            outb[k, pl.ds(rows, CROWS), :] = outf[pl.ds(pl.multiple_of(k * INNER + rows, 8), CROWS), :].astype(BF16)
-        for d in range(1, ROW):
-            ocopy(c, d, g).start()
+    for first, count, s in late:
+        if count:
+            tacc[pl.ds(first, count)] += through(first, count, s)
+    pl.when(has_part[0])(shift_start)
+    finish(1, tacc[CHUNK : 2 * CHUNK].reshape(CHUNK * ROW * ROW, BLOCK))
+
+    def product(n, _):
+        c = n * 2
+        acc = tacc[pl.ds(c * CHUNK, CHUNK)]
+        for s in range(1, SLOTS):
+            acc += through(c * CHUNK, CHUNK, s)
+
+        @pl.when(n == 1)
+        def _():
+            shift_pass()
+            lax.fori_loop(0, CHUNKS - 1, emit, 0)
+
+        finish(c, acc.reshape(CHUNK * ROW * ROW, BLOCK))
         return 0
 
-    lax.fori_loop(0, CHUNKS, product, 0)
+    lax.fori_loop(0, 2, product, 0)
+    emit(CHUNKS - 1, 0)
 
     own = outf[pl.ds(pl.multiple_of(g * INNER, 8), INNER), :]
     for d in range(1, ROW):
@@ -345,6 +380,7 @@
             pltpu.VMEM((PARTS * 2 * PART, LANES), F32),
             pltpu.VMEM((2 * BLOCKS, Z * ROW, BLOCK), BF16),
             pltpu.VMEM((2 * BLOCKS, ROW, BLOCK), F32),
+            pltpu.VMEM((BLOCKS, ROW * ROW, BLOCK), F32),
             pltpu.VMEM((SLOTS, BLOCK, BLOCK), BF16),
             pltpu.VMEM((ROW * INNER, LANES), F32),
             pltpu.VMEM((ROW, INNER, LANES), BF16),

time: 65.9 us -> 66.1 us (level)
  no operation moved by 1% of the time
where the time goes in v3:
time: 66.1 us; the launch traced here: 65.8 us
  Pallas kernels  62.8 us (95%)
  other arithmetic  1.54 us (2%)
  local copies, waits for them, and re-layouts  1.42 us (2%)
    pallas_call x1, Pallas kernels, on_device(): pl.pallas_call(kernel, out_shape=jax.ShapeDtypeStruct((INNER, LANES), F32...  62.8 us
    unnamed x1, other arithmetic  1.54 us
    unnamed x1, local copies, waits for them, and re-layouts  1.42 us

profile of v3, /device:TPU:1, one launch (start us, length us, event | category | flops | bytes accessed | tf_op | source)
XLA Modules:
  0.0 65.8 jit_solution(2517885833727090244)
XLA Ops:
  0.0 1.5 %reduce = bf16[12288]{0:T(1024)(128)(2,1)} reduce(bf16[1,12288]{1,0:T(2,128)(2,1)} %param.5, bf16[]{:T(256)} %constant.2), dimensions={0}, to_apply=%param.5.reduce_sub_computation | reduce | bytes 49154 | tf_op args[1]
  1.5 62.8 %covariance.1 = f32[96,128]{1,0:T(8,128)} custom-call(f32[96,128]{1,0:T(8,128)} %bitcast.6, bf16[96,128]{1,0:T(8,128)(2,1)} %bitcast.5, s32[7,24]{1,0:T(8,128)} %bitcast.7, bf16[8,512,512]{2,1,0:T(8,128)(2,1)} %tap_hbm.1), custom_call_target="tpu_custom_call" | custom-call | tf_op jit(solution)/shard_map/covariance/pallas_call | solution.py:366
  64.4 1.4 %copy.6 = f32[1,12288]{1,0:T(1,128)} copy(f32[1,12288]{1,0:T(1,128)} %bitcast.4) | data formatting | bytes 98304

commit v4 on v3

--- a/solution.py
+++ b/solution.py
@@ -157,11 +157,11 @@
             return (rk > rank_me) if late else (rk <= rank_me)
 
         for dl, d, dev, rk in far:
+            if dl in dls:
+                pl.when(due(rk) & has_part[dl])(lambda: mcopy(abs(dl), d, zlo, dev).start())
+        for dl, d, dev, rk in far:
             if dl in dls and d % 2 == 0:
                 pl.when(due(rk))(lambda: dcopy(dl, d, zq, dev).start())
-        for dl, d, dev, rk in far:
-            if dl in dls:
-                pl.when(due(rk) & has_part[dl])(lambda: mcopy(abs(dl), d, zlo, dev).start())
 
     send_far(False, (1, -1))
     send_far(False, (0,))
@@ -232,18 +232,6 @@
         inner = [i for i in mid if BLOCKS // 2 + 1 - s <= i <= BLOCKS // 2 + 6 - s]
         tacc[pl.ds(inner[0], len(inner))] += through(inner[0], len(inner), s)
         late += [(mid[0], inner[0] - mid[0], s), (inner[-1] + 1, mid[-1] - inner[-1], s)]
-
-    for dl in (1, -1):
-        for k in range(HALF):
-            dcopy(dl, 0, k, far[0][2]).wait_recv()
-        bcopy(1 if dl == 1 else 2, core).start()
-    widen(db, df, core * HALF, HALF, 0, RIM)
-    widen(db, df, core * HALF, HALF, RIM + INNER, RIM)
-    for n in (1, 2):
-        bcopy(n, 1 - core).wait_recv()
-        lo = (n - 1) * (RIM + INNER)
-        widen(db, df, (1 - core) * HALF, HALF, lo, RIM)
-        lax.fori_loop(lo // Q, lo // Q + BLOCKS // 2, weigh, 0)
 
     def shift_start():
         for k in range(Z):
@@ -286,6 +274,20 @@
                 outf[pl.ds(i * Q + q, ROW, stride=INNER), :] += (
                     shift * acc[i * ROW : (i + 1) * ROW, q * LANES : (q + 1) * LANES]
                 )
+
+    pl.when(has_part[0])(shift_start)
+    for dl in (1, -1):
+        for k in range(HALF):
+            dcopy(dl, 0, k, far[0][2]).wait_recv()
+        bcopy(1 if dl == 1 else 2, core).start()
+    shift_pass()
+    widen(db, df, core * HALF, HALF, 0, RIM)
+    widen(db, df, core * HALF, HALF, RIM + INNER, RIM)
+    for n in (1, 2):
+        bcopy(n, 1 - core).wait_recv()
+        lo = (n - 1) * (RIM + INNER)
+        widen(db, df, (1 - core) * HALF, HALF, lo, RIM)
+        lax.fori_loop(lo // Q, lo // Q + BLOCKS // 2, weigh, 0)
 
     def emit(c, _):
         rows = pl.multiple_of(c * CROWS, CROWS)
@@ -308,25 +310,19 @@
     for first, count, s in late:
         if count:
             tacc[pl.ds(first, count)] += through(first, count, s)
-    pl.when(has_part[0])(shift_start)
     finish(1, tacc[CHUNK : 2 * CHUNK].reshape(CHUNK * ROW * ROW, BLOCK))
+    emit(1, 0)
 
     def product(n, _):
         c = n * 2
         acc = tacc[pl.ds(c * CHUNK, CHUNK)]
         for s in range(1, SLOTS):
             acc += through(c * CHUNK, CHUNK, s)
-
-        @pl.when(n == 1)
-        def _():
-            shift_pass()
-            lax.fori_loop(0, CHUNKS - 1, emit, 0)
-
         finish(c, acc.reshape(CHUNK * ROW * ROW, BLOCK))
+        emit(c, 0)
         return 0
 
     lax.fori_loop(0, 2, product, 0)
-    emit(CHUNKS - 1, 0)
 
     own = outf[pl.ds(pl.multiple_of(g * INNER, 8), INNER), :]
     for d in range(1, ROW):

time: 66.1 us -> 68.5 us (1.036)
  Pallas kernels: 62.8 us -> 65.3 us
    pallas_call x1, Pallas kernels: 62.8 us -> 65.3 us  [on_device(): pl.pallas_call(kernel, out_shape=jax.ShapeDtypeStruct((INNER, LANES), F32...]
where the time goes in v4:
time: 68.5 us; the launch traced here: 68.2 us
  Pallas kernels  65.3 us (95%)
  other arithmetic  1.54 us (2%)
  local copies, waits for them, and re-layouts  1.42 us (2%)
    pallas_call x1, Pallas kernels, on_device(): pl.pallas_call(kernel, out_shape=jax.ShapeDtypeStruct((INNER, LANES), F32...  65.3 us
    unnamed x1, other arithmetic  1.54 us
    unnamed x1, local copies, waits for them, and re-layouts  1.42 us

profile of v4, /device:TPU:1, one launch (start us, length us, event | category | flops | bytes accessed | tf_op | source)
XLA Modules:
  0.0 68.2 jit_solution(4372521130086970837)
XLA Ops:
  0.0 1.5 %reduce = bf16[12288]{0:T(1024)(128)(2,1)} reduce(bf16[1,12288]{1,0:T(2,128)(2,1)} %param.5, bf16[]{:T(256)} %constant.2), dimensions={0}, to_apply=%param.5.reduce_sub_computation | reduce | bytes 49154 | tf_op args[1]
  1.5 65.3 %covariance.1 = f32[96,128]{1,0:T(8,128)} custom-call(f32[96,128]{1,0:T(8,128)} %bitcast.6, bf16[96,128]{1,0:T(8,128)(2,1)} %bitcast.5, s32[7,24]{1,0:T(8,128)} %bitcast.7, bf16[8,512,512]{2,1,0:T(8,128)(2,1)} %tap_hbm.1), custom_call_target="tpu_custom_call" | custom-call | tf_op jit(solution)/shard_map/covariance/pallas_call | solution.py:362
  66.8 1.4 %copy.6 = f32[1,12288]{1,0:T(1,128)} copy(f32[1,12288]{1,0:T(1,128)} %bitcast.4) | data formatting | bytes 98304
